TPU v7x, 32 devices: a whole 2x2x4 slice. The times are simulated.
32 devices in a mesh: gz: 4 (over y, x), row: 2 (over core), col: 4 (over z).
Axes of the slice: x: 2, y: 2, z: 4, core: 2. Of those that a mesh axis runs over, the one named last changes fastest.
Arguments:
- leaf_probe: bfloat16 [32, 512, 128], P(('gz', 'row', 'col')), may hold values from -6 to 6
- leaf_lower_inv: bfloat16 [32, 512, 512], P(('gz', 'row', 'col')), may hold values from -0.25 to 0.25
- leaf_upper_inv: bfloat16 [32, 512, 512], P(('gz', 'row', 'col')), may hold values from -0.25 to 0.25
- leaf_lower_panel: bfloat16 [32, 1024, 512], P(('gz', 'row', 'col')), may hold values from -0.09375 to 0.09375
- leaf_upper_panel: bfloat16 [32, 512, 1024], P(('gz', 'row', 'col')), may hold values from -0.1875 to 0.1875
- leaf_tiles: int32 [32], P(('gz', 'row', 'col')), may hold values from 1 to 4, as said below
- coupled: int32 [32, 8], P(('gz', 'row', 'col')), may hold values from 0 to 31, as said below
- top_probe: bfloat16 [4, 1024, 128], P(None, ('row', 'col')), may hold values from -6 to 6
- top_lower_inv: bfloat16 [4, 1024, 1024], P(None, ('row', 'col')), may hold values from -0.1875 to 0.1875
- top_lower_blocks: bfloat16 [6, 1024, 1024], P(None, ('row', 'col')), may hold values from -0.125 to 0.125
- top_upper_inv: bfloat16 [4, 1024, 1024], P(None, ('row', 'col')), may hold values from -0.1875 to 0.1875
- top_upper_blocks: bfloat16 [6, 1024, 1024], P(None, ('row', 'col')), may hold values from -0.125 to 0.125
Outputs:
- leaf_solution: float32 [32, 512, 128], P(('gz', 'row', 'col'))
- top_solution: float32 [4, 1024, 128], P(None, ('row', 'col'))
Inputs may be any that keep to these rules, and one draw needn't show every extreme that they name: `leaf_tiles`: some leaf has 4 blocks. `coupled`: the 8 numbers of one leaf are distinct.
All inputs are finite; a program needn't handle non-finite values.
Results may differ from a plain program's by a relative error of at most 0.02.
Values may be sent and summed in bfloat16 or wider, within the bound.
A program may use at most 128 MiB of HBM per device.

v0:
```python
import jax
import jax.numpy as jnp
from jax import lax
from jax.sharding import PartitionSpec as P

TILE = 128


def pair_index(higher, lower):
    return higher * (higher - 1) // 2 + lower


def live_rows(live_tiles, length):
    return (lax.iota(jnp.int32, length) < live_tiles * TILE)[:, None]


def solve_level(inverse, target):
    return jnp.dot(
        inverse,
        lax.all_gather(target, ("row", "col"), axis=0, tiled=True),
        preferred_element_type=jnp.float32,
    )


def gather_level(values):
    return lax.all_gather(values, ("row", "col"), axis=0, tiled=True)


def layer_reduce(partial_value):
    return lax.psum(partial_value.astype(jnp.bfloat16), "gz").astype(jnp.float32)


def body(
    leaf_probe,
    leaf_lower_inv,
    leaf_upper_inv,
    leaf_lower_panel,
    leaf_upper_panel,
    leaf_tiles,
    coupled,
    top_probe,
    top_lower_inv,
    top_lower_blocks,
    top_upper_inv,
    top_upper_blocks,
):
    leaf_width = leaf_probe.shape[1]
    columns = leaf_probe.shape[2]
    levels = top_probe.shape[0]
    sep_total = top_lower_inv.shape[2]
    tile_count = levels * sep_total // TILE
    update = jnp.zeros((tile_count, TILE, columns), jnp.float32)
    leaf_index = 0
    live_mask = live_rows(leaf_tiles[leaf_index], leaf_width)
    masked = jnp.where(live_mask, leaf_probe[leaf_index], jnp.zeros_like(leaf_probe[leaf_index]))
    solved = jnp.where(
        live_mask,
        jnp.dot(leaf_lower_inv[leaf_index], masked, preferred_element_type=jnp.float32),
        0.0,
    ).astype(jnp.bfloat16)
    forward_leaves = [solved]
    contribution = jnp.dot(
        leaf_lower_panel[leaf_index], solved, preferred_element_type=jnp.float32
    ).reshape(-1, TILE, columns)
    update = update.at[coupled[leaf_index]].add(contribution)
    update = update.reshape(levels, sep_total, columns)
    shares = lax.psum_scatter(
        update.astype(jnp.bfloat16), ("row", "col"), scatter_dimension=1, tiled=True
    ).astype(jnp.float32)
    gathered = []
    forward_top = []
    for level in range(levels):
        level_share = shares[level]
        target = top_probe[level].astype(jnp.float32) - layer_reduce(level_share)
        for other in range(level):
            target = target - jnp.dot(
                top_lower_blocks[pair_index(level, other)],
                gathered[other],
                preferred_element_type=jnp.float32,
            )
        solved = solve_level(top_lower_inv[level], target.astype(jnp.bfloat16)).astype(jnp.bfloat16)
        forward_top.append(solved)
        if level + 1 < levels:
            gathered.append(gather_level(solved))
    whole_levels = [None] * levels
    top_parts = [None] * levels
    for level in range(levels - 1, -1, -1):
        target = forward_top[level].astype(jnp.float32)
        for other in range(levels - 1, level, -1):
            target = target - jnp.dot(
                top_upper_blocks[pair_index(other, level)],
                whole_levels[other],
                preferred_element_type=jnp.float32,
            )
        solution = solve_level(top_upper_inv[level], target.astype(jnp.bfloat16))
        top_parts[level] = solution
        whole_levels[level] = gather_level(solution.astype(jnp.bfloat16))
    whole_top = jnp.concatenate(whole_levels, 0).reshape(tile_count, TILE, columns)
    leaf_index = 0
    live_mask = live_rows(leaf_tiles[leaf_index], leaf_width)
    picked = whole_top[coupled[leaf_index]].reshape(-1, columns)
    target = forward_leaves[leaf_index].astype(jnp.float32) - jnp.dot(
        leaf_upper_panel[leaf_index], picked, preferred_element_type=jnp.float32
    )
    target = jnp.where(live_mask, target, 0.0).astype(jnp.bfloat16)
    leaf_parts = [
        jnp.where(
            live_mask,
            jnp.dot(leaf_upper_inv[leaf_index], target, preferred_element_type=jnp.float32),
            0.0,
        )
    ]
    return (jnp.stack(leaf_parts), jnp.stack(top_parts))


def solution(mesh):
    return jax.shard_map(
        body,
        mesh=mesh,
        in_specs=(
            P(("gz", "row", "col"), None, None),
            P(("gz", "row", "col"), None, None),
            P(("gz", "row", "col"), None, None),
            P(("gz", "row", "col"), None, None),
            P(("gz", "row", "col"), None, None),
            P(("gz", "row", "col")),
            P(("gz", "row", "col"), None),
            P(None, ("row", "col"), None),
            P(None, ("row", "col"), None),
            P(None, ("row", "col"), None),
            P(None, ("row", "col"), None),
            P(None, ("row", "col"), None),
        ),
        out_specs=(P(("gz", "row", "col"), None, None), P(None, ("row", "col"), None)),
        check_vma=False,
    )
```

profile of v0, /device:TPU:0, one launch (start us, length us, event | category | flops | bytes accessed | tf_op | source)
XLA Modules:
  0.0 474.1 jit_solution(14166314018123281131)
XLA Ops:
  8.0 1.6 fusion.2
  9.6 0.5 convolution_bitcast_fusion
  10.0 1.0 copy.20
  11.3 2.0 scatter_fusion
  13.3 1.1 convert_element_type.142
  14.5 38.4 %reduce-scatter.2.cloned.1.call-done = bf16[4,128,128]{2,1,0:T(8,128)(2,1)} async-done(((bf16[4,1024,128]{2,1,0:T(8,128)(2,1)}), bf16[4,128,128]{2,1,0:T(8,128)(2,1)}) %reduce-scatter.2.cloned.1.call-update) | async-done | bytes 131088 | tf_op jit(solution)/shard_map/reduce_scatter | solution.py:67
  52.9 1.4 slice_bitcast_fusion
  54.4 43.7 %all-reduce.3.cloned.1.call-done = (bf16[128,128]{1,0:T(8,128)(2,1)}, bf16[128,128]{1,0:T(8,128)(2,1)}, bf16[128,128]{1,0:T(8,128)(2,1)}, bf16[128,128]{1,0:T(8,128)(2,1)}) async-done(((bf16[128,128]{1,0:T(8,128)(2,1)}, bf16[128,128]{1,0:T(8,128)(2,1)}, bf16[128,128]{1,0:T(8,128)(2,1)}, bf16[128,128]{1,0:T(8,128)(2,1)}), (bf16[128,128]{1,0:T(8,128)(2,1)}, bf16[128,128]{1,0:T(8,128)(2,1)}, ...) | async-done | bytes 131088 | tf_op jit(solution)/shard_map/psum | solution.py:30
  98.1 0.9 fusion.81
  99.0 25.3 %all_gather.45 = bf16[1024,128]{1,0:T(8,128)(2,1)S(1)} all-gather(bf16[128,128]{1,0:T(8,128)(2,1)S(1)} %fusion.81), channel_id=1, replica_groups=mesh['gz'=4,'row'=2,'col'=4] {'row','col'}, dimensions={0}, use_global_device_ids=true | all-gather | bytes 294912 | tf_op jit(solution)/shard_map/all_gather | solution.py:20
  124.3 1.2 fusion.22
  125.5 22.7 %all_gather.46 = bf16[1024,128]{0,1:T(8,128)(2,1)S(1)} all-gather(bf16[128,128]{0,1:T(8,128)(2,1)S(1)} %fusion.22), channel_id=1, replica_groups=mesh['gz'=4,'row'=2,'col'=4] {'row','col'}, dimensions={0}, use_global_device_ids=true | all-gather | bytes 294912 | tf_op jit(solution)/shard_map/all_gather | solution.py:26
  148.2 1.0 fusion.16
  149.2 25.2 %all_gather.47 = bf16[1024,128]{1,0:T(8,128)(2,1)S(1)} all-gather(bf16[128,128]{1,0:T(8,128)(2,1)S(1)} %fusion.16), channel_id=1, replica_groups=mesh['gz'=4,'row'=2,'col'=4] {'row','col'}, dimensions={0}, use_global_device_ids=true | all-gather | bytes 294912 | tf_op jit(solution)/shard_map/all_gather | solution.py:20
  174.4 0.3 fusion.23
  174.7 22.6 %all_gather.48 = bf16[1024,128]{0,1:T(8,128)(2,1)S(1)} all-gather(bf16[128,128]{0,1:T(8,128)(2,1)S(1)} %fusion.23), channel_id=1, replica_groups=mesh['gz'=4,'row'=2,'col'=4] {'row','col'}, dimensions={0}, use_global_device_ids=true | all-gather | bytes 294912 | tf_op jit(solution)/shard_map/all_gather | solution.py:26
  197.7 25.2 %all_gather.49 = bf16[1024,128]{1,0:T(8,128)(2,1)S(1)} all-gather(bf16[128,128]{1,0:T(8,128)(2,1)S(1)} %fusion.17), channel_id=1, replica_groups=mesh['gz'=4,'row'=2,'col'=4] {'row','col'}, dimensions={0}, use_global_device_ids=true | all-gather | bytes 294912 | tf_op jit(solution)/shard_map/all_gather | solution.py:20
  223.2 23.1 %all_gather.50 = bf16[1024,128]{0,1:T(8,128)(2,1)S(1)} all-gather(bf16[128,128]{0,1:T(8,128)(2,1)S(1)} %fusion.24), channel_id=1, replica_groups=mesh['gz'=4,'row'=2,'col'=4] {'row','col'}, dimensions={0}, use_global_device_ids=true | all-gather | bytes 294912 | tf_op jit(solution)/shard_map/all_gather | solution.py:26
  247.0 25.4 %all_gather.51 = bf16[1024,128]{1,0:T(8,128)(2,1)S(1)} all-gather(bf16[128,128]{1,0:T(8,128)(2,1)S(1)} %fusion.18), channel_id=1, replica_groups=mesh['gz'=4,'row'=2,'col'=4] {'row','col'}, dimensions={0}, use_global_device_ids=true | all-gather | bytes 294912 | tf_op jit(solution)/shard_map/all_gather | solution.py:20
  272.7 23.1 %all_gather.52 = bf16[1024,128]{0,1:T(8,128)(2,1)S(1)} all-gather(bf16[128,128]{0,1:T(8,128)(2,1)S(1)} %fusion.25), channel_id=1, replica_groups=mesh['gz'=4,'row'=2,'col'=4] {'row','col'}, dimensions={0}, use_global_device_ids=true | all-gather | bytes 294912 | tf_op jit(solution)/shard_map/all_gather | solution.py:20
  296.0 23.2 %all_gather.53 = bf16[1024,128]{0,1:T(8,128)(2,1)S(1)} all-gather(bf16[128,128]{0,1:T(8,128)(2,1)S(1)} %get-tuple-element.14), channel_id=1, replica_groups=mesh['gz'=4,'row'=2,'col'=4] {'row','col'}, dimensions={0}, use_global_device_ids=true | all-gather | bytes 294912 | tf_op jit(solution)/shard_map/all_gather | solution.py:26
  319.9 23.2 %all_gather.54 = bf16[1024,128]{0,1:T(8,128)(2,1)S(1)} all-gather(bf16[128,128]{0,1:T(8,128)(2,1)S(1)} %fusion.19), channel_id=1, replica_groups=mesh['gz'=4,'row'=2,'col'=4] {'row','col'}, dimensions={0}, use_global_device_ids=true | all-gather | bytes 294912 | tf_op jit(solution)/shard_map/all_gather | solution.py:20
  343.3 23.2 %all_gather.55 = bf16[1024,128]{0,1:T(8,128)(2,1)S(1)} all-gather(bf16[128,128]{0,1:T(8,128)(2,1)S(1)} %get-tuple-element.16), channel_id=1, replica_groups=mesh['gz'=4,'row'=2,'col'=4] {'row','col'}, dimensions={0}, use_global_device_ids=true | all-gather | bytes 294912 | tf_op jit(solution)/shard_map/all_gather | solution.py:26
  367.0 23.2 %all_gather.56 = bf16[1024,128]{0,1:T(8,128)(2,1)S(1)} all-gather(bf16[128,128]{0,1:T(8,128)(2,1)S(1)} %fusion.20), channel_id=1, replica_groups=mesh['gz'=4,'row'=2,'col'=4] {'row','col'}, dimensions={0}, use_global_device_ids=true | all-gather | bytes 294912 | tf_op jit(solution)/shard_map/all_gather | solution.py:20
  390.5 23.1 %all_gather.57 = bf16[1024,128]{0,1:T(8,128)(2,1)S(1)} all-gather(bf16[128,128]{0,1:T(8,128)(2,1)S(1)} %get-tuple-element.18), channel_id=1, replica_groups=mesh['gz'=4,'row'=2,'col'=4] {'row','col'}, dimensions={0}, use_global_device_ids=true | all-gather | bytes 294912 | tf_op jit(solution)/shard_map/all_gather | solution.py:26
  413.9 23.0 %all_gather.58 = bf16[1024,128]{0,1:T(8,128)(2,1)S(1)} all-gather(bf16[128,128]{0,1:T(8,128)(2,1)S(1)} %fusion.21), channel_id=1, replica_groups=mesh['gz'=4,'row'=2,'col'=4] {'row','col'}, dimensions={0}, use_global_device_ids=true | all-gather | bytes 294912 | tf_op jit(solution)/shard_map/all_gather | solution.py:20
  437.2 0.8 copy.19
  438.0 23.2 %all_gather.59 = bf16[1024,128]{0,1:T(8,128)(2,1)S(1)} all-gather(bf16[128,128]{0,1:T(8,128)(2,1)S(1)} %get-tuple-element.20), channel_id=1, replica_groups=mesh['gz'=4,'row'=2,'col'=4] {'row','col'}, dimensions={0}, use_global_device_ids=true | all-gather | bytes 294912 | tf_op jit(solution)/shard_map/all_gather | solution.py:26
  461.4 1.3 copy.21
  462.7 1.8 gather_fusion
  464.5 1.9 fusion
  466.4 0.8 copy.18
  (47 shorter events, 4.5 us)
Async XLA Ops:
  7.2 2.4 copy-start
  7.2 45.7 %reduce-scatter.2.cloned.1.call-start = ((), (), s32[]{:S(2)}) async-start(), calls=%async_computation.1 | async-start | bytes 1179648 | tf_op jit(solution)/shard_map/reduce_scatter | solution.py:67
  9.5 1.5 copy-start.9
  13.3 84.8 %copy-start.6 = (bf16[4,128,128]{2,1,0:T(8,128)(2,1)S(1)}, bf16[4,128,128]{2,1,0:T(8,128)(2,1)}, u32[]{:S(2)}) copy-start(bf16[4,128,128]{2,1,0:T(8,128)(2,1)} %param.19) | copy-start | bytes 393220
  14.5 133.7 %copy-start.2 = (bf16[6,128,1024]{2,1,0:T(8,128)(2,1)S(1)}, bf16[6,128,1024]{2,1,0:T(8,128)(2,1)}, u32[]{:S(2)}) copy-start(bf16[6,128,1024]{2,1,0:T(8,128)(2,1)} %param.21) | copy-start | bytes 4718596
  14.5 83.6 %all-reduce.3.cloned.1.call-start = ((), (), s32[]{:S(2)}) async-start(), calls=%async_computation.2 | async-start | bytes 262144 | tf_op jit(solution)/shard_map/psum | solution.py:30
  98.1 76.3 %copy-start.3 = (bf16[4,128,1024]{2,1,0:T(8,128)(2,1)S(1)}, bf16[4,128,1024]{2,1,0:T(8,128)(2,1)}, u32[]{:S(2)}) copy-start(bf16[4,128,1024]{2,1,0:T(8,128)(2,1)} %param.20) | copy-start | bytes 3145732
  98.1 99.1 %copy-start.8 = (bf16[128,128]{1,0:T(8,128)(2,1)S(1)}, bf16[128,128]{1,0:T(8,128)(2,1)}, u32[]{:S(2)}) copy-start(bf16[128,128]{1,0:T(8,128)(2,1)} %get-tuple-element.9) | copy-start | bytes 98308
  174.4 71.9 %copy-start.7 = (bf16[128,128]{1,0:T(8,128)(2,1)S(1)}, bf16[128,128]{1,0:T(8,128)(2,1)}, u32[]{:S(2)}) copy-start(bf16[128,128]{1,0:T(8,128)(2,1)} %get-tuple-element.7) | copy-start | bytes 98308
  246.3 49.4 %copy-start.4 = (bf16[4,128,1024]{2,1,0:T(8,128)(2,1)S(1)}, bf16[4,128,1024]{2,1,0:T(8,128)(2,1)}, u32[]{:S(2)}) copy-start(bf16[4,128,1024]{2,1,0:T(8,128)(2,1)} %param.22) | copy-start | bytes 3145732
  246.5 72.6 %copy-start.1 = (bf16[6,128,1024]{2,1,0:T(8,128)(2,1)S(1)}, bf16[6,128,1024]{2,1,0:T(8,128)(2,1)}, u32[]{:S(2)}) copy-start(bf16[6,128,1024]{2,1,0:T(8,128)(2,1)} %param.23) | copy-start | bytes 4718596
  461.3 3.2 copy-start.5
Sparse Core Ops, SparseCore 0:
  14.6 38.2 reduce-scatter.1
  56.5 41.5 all-reduce.2
where the time goes:
time: 475 us; the launch traced here: 474 us
  blocking collectives  355 us (75%)
  waiting for transfers between devices  82.1 us (17%)
  between operations  15 us (3%)
  matrix products  10.4 us (2%)
  local copies, waits for them, and re-layouts  7.53 us (2%)
    all_gather x8, blocking collectives, solve_level(): lax.all_gather(target, ('row', 'col'), axis=0, tiled=True)  194 us
    all_gather x7, blocking collectives, gather_level(): return lax.all_gather(values, ('row', 'col'), axis=0, tiled=True)  161 us
    psum x1, waiting for transfers between devices, layer_reduce(): lax.psum(partial_value.astype(jnp.bfloat16), 'gz').astype(jnp.float32)  43.7 us
    reduce_scatter x1, waiting for transfers between devices, body(): lax.psum_scatter(update.astype(jnp.bfloat16), ('row', 'col'), scatter_dim...  38.4 us
  transfers between devices with their start and end apart: 2, of which 2 were waited for; matrix products, arithmetic and copies ran while one was open for 0% of the time, Pallas kernels for 0%

commit v1 on v0

v1 whole, which is shorter than its diff:
```python
import functools

import jax
import jax.numpy as jnp
from jax import lax
from jax.experimental import pallas as pl
from jax.experimental.pallas import tpu as pltpu
from jax.sharding import PartitionSpec as P

TILE = 128
F32 = jnp.float32
BF16 = jnp.bfloat16


def pair_index(higher, lower):
    return higher * (higher - 1) // 2 + lower


def dot_t(left, right):
    return lax.dot_general(left, right, (((1,), (1,)), ((), ())), preferred_element_type=F32)


def kernel(
    sizes,
    tiles_ref,
    coupled_ref,
    leaf_probe_hbm,
    leaf_lower_inv_hbm,
    leaf_lower_panel_hbm,
    top_probe_hbm,
    top_lower_inv_hbm,
    top_lower_blocks_hbm,
    top_upper_inv_hbm,
    top_upper_blocks_hbm,
    leaf_upper_panel_hbm,
    leaf_upper_inv_hbm,
    leaf_out,
    top_out,
    leaf_probe,
    leaf_lower_inv,
    leaf_lower_panel,
    top_probe,
    top_lower_inv,
    top_lower_blocks,
    top_upper_inv,
    top_upper_blocks,
    leaf_upper_panel,
    leaf_upper_inv,
    solved_t,
    blocks_t,
    probe_t,
    upd,
    row_in,
    row_sum,
    gz_in,
    gz_sum,
    col_in,
    rings,
    whole,
    load_sem,
    row_sems,
    gz_sems,
    col_sems,
    gather_sems,
    whole_sems,
):
    levels, n_gz, n_row, n_col, part, couplings, leaf_width = sizes
    group = n_row * n_col
    g, r, c = lax.axis_index("gz"), lax.axis_index("row"), lax.axis_index("col")
    d = r * n_col + c
    forward_steps = 2 * levels - 1

    sources = [
        (leaf_probe_hbm, leaf_probe),
        (leaf_lower_inv_hbm, leaf_lower_inv),
        (leaf_lower_panel_hbm, leaf_lower_panel),
        (top_probe_hbm, top_probe),
        (top_lower_inv_hbm, top_lower_inv),
        (top_lower_blocks_hbm, top_lower_blocks),
        (top_upper_inv_hbm, top_upper_inv),
        (top_upper_blocks_hbm, top_upper_blocks),
        (leaf_upper_panel_hbm, leaf_upper_panel),
        (leaf_upper_inv_hbm, leaf_upper_inv),
    ]
    loads = [
        pltpu.make_async_copy(src, dst, load_sem.at[i]) for i, (src, dst) in enumerate(sources)
    ]
    for load in loads:
        load.start()

    def each(count, step):
        lax.fori_loop(1, count, lambda i, carry: (step(i), carry)[1], 0, unroll=count <= 8)

    barrier = pltpu.get_barrier_semaphore()

    def group_peer(i):
        peer = lax.rem(d + i, group)
        return (g, lax.div(peer, n_col), lax.rem(peer, n_col))

    def gz_peer(i):
        return (lax.rem(g + i, n_gz), r, c)

    def greet(device):
        pl.semaphore_signal(barrier, inc=1, device_id=device, device_id_type=pl.DeviceIdType.MESH)

    each(group, lambda i: greet(group_peer(i)))
    each(n_gz, lambda i: greet(gz_peer(i)))

    def send(src, dst, sems, at, device):
        pltpu.make_async_remote_copy(
            src_ref=src,
            dst_ref=dst,
            send_sem=sems.at[0, at],
            recv_sem=sems.at[1, at],
            device_id=device,
            device_id_type=pl.DeviceIdType.MESH,
        ).start()

    def wait_bytes(ref, sem):
        pltpu.make_async_copy(ref, ref, sem).wait()

    def row_send(a):
        def step(i):
            other = lax.rem(r + i, n_row)
            send(upd.at[a, other], row_in.at[a, r], row_sems, a, (g, other, c))

        each(n_row, step)

    def row_finish(a):
        if n_row > 1:
            wait_bytes(row_in.at[a, pl.ds(0, n_row - 1)], row_sems.at[1, a])
        total = upd[a, r].astype(F32)
        for i in range(1, n_row):
            total = total + row_in[a, lax.rem(r + i, n_row)].astype(F32)
        row_sum[a] = total.astype(BF16)

    def gz_send(a):
        def step(i):
            other = lax.rem(g + i, n_gz)
            send(row_sum.at[a, other], gz_in.at[a, g], gz_sems, a, (other, r, c))

        each(n_gz, step)

    def gz_finish(a):
        if n_gz > 1:
            wait_bytes(gz_in.at[a, pl.ds(0, n_gz - 1)], gz_sems.at[1, a])
        total = row_sum[a, g].astype(F32)
        for i in range(1, n_gz):
            total = total + gz_in[a, lax.rem(g + i, n_gz)].astype(F32)
        gz_sum[a] = total.astype(BF16)

    def col_send(a):
        def step(i):
            other = lax.rem(c + i, n_col)
            send(gz_sum.at[a, other], col_in.at[a, c], col_sems, a, (g, r, other))

        each(n_col, step)

    def col_finish(a):
        if n_col > 1:
            wait_bytes(col_in.at[a, pl.ds(0, n_col - 1)], col_sems.at[1, a])
        total = gz_sum[a, c].astype(F32)
        for i in range(1, n_col):
            total = total + col_in[a, lax.rem(c + i, n_col)].astype(F32)
        return probe_t[a, g] - total

    def gather_send(step_at, value):
        rings[step_at, d] = value

        def step(i):
            send(rings.at[step_at, d], rings.at[step_at, d], gather_sems, step_at, group_peer(i))

        each(group, step)

    def gather_wait(step_at):
        if group > 1:
            wait_bytes(rings.at[step_at, pl.ds(0, group - 1)], gather_sems.at[1, step_at])
        return jnp.concatenate([rings[step_at, i] for i in range(group)], axis=1)

    def solved_send(a, value):
        at = a * group + d
        whole[g, at] = value

        def step(i):
            send(whole.at[g, at], whole.at[g, at], gather_sems, 3 * levels - 1 + a, group_peer(i))

        each(group, step)

    def solved_wait(a):
        if group > 1:
            wait_bytes(
                whole.at[g, pl.ds(a * group, group - 1)], gather_sems.at[1, 3 * levels - 1 + a]
            )
        return jnp.concatenate([whole[g, a * group + i] for i in range(group)], axis=1)

    def whole_send(a):
        def step(i):
            at = pl.ds(a * group, group)
            send(whole.at[g, at], whole.at[g, at], whole_sems, a, gz_peer(i))

        each(n_gz, step)

    def whole_wait(a):
        if n_gz > 1:
            wait_bytes(whole.at[pl.ds(0, n_gz - 1), pl.ds(a * group, group)], whole_sems.at[1, a])

    live = lax.broadcasted_iota(jnp.int32, (1, leaf_width), 1) < tiles_ref[0] * TILE
    loads[0].wait()
    masked = jnp.where(live, leaf_probe[0].astype(F32).T, 0.0).astype(BF16)
    loads[1].wait()
    solved = jnp.where(live, dot_t(masked, leaf_lower_inv[0]), 0.0).astype(BF16)
    solved_t[...] = solved
    loads[2].wait()
    for j in range(couplings):
        rows = leaf_lower_panel[0, pl.ds(j * TILE, TILE), :]
        blocks_t[j] = dot_t(solved, rows).astype(BF16)
    blocks_t[couplings] = jnp.zeros(blocks_t.shape[1:], BF16)

    def spread(a):
        def place(t, carry):
            at = jnp.int32(couplings)
            for j in range(couplings):
                at = jnp.where(coupled_ref[0, j] == a * group + t, j, at)
            block = blocks_t[at]
            t_row, t_col = lax.div(t, n_col), lax.rem(t, n_col)
            for k in range(n_gz):
                upd[a, t_row, k, t_col] = block[k * part : (k + 1) * part]
            return carry

        lax.fori_loop(0, group, place, 0)

    spread(0)
    pl.semaphore_wait(barrier, group - 1 + n_gz - 1)
    row_send(0)
    for a in range(1, levels):
        spread(a)
        row_send(a)
    row_finish(0)
    gz_send(0)
    loads[3].wait()
    for a in range(levels):
        probe_t[a] = top_probe[a].astype(F32).T.reshape(probe_t.shape[1:])
    for a in range(1, levels):
        row_finish(a)
        gz_send(a)
    gz_finish(0)
    col_send(0)
    loads[4].wait()
    loads[5].wait()
    target = {0: col_finish(0)}

    forward = []
    for a in range(levels):
        gather_send(2 * a, target[a].astype(BF16))
        if a + 1 < levels:
            gz_finish(a + 1)
            col_send(a + 1)
        if a >= 1:
            for h in range(a + 1, levels):
                known = [l for l in range(levels) if l == a - 1]
                for l in known:
                    pending[h] = pending.get(h, 0.0) + dot_t(gathered[l], top_lower_blocks[pair_index(h, l)])
        else:
            gathered = []
            pending = {}
        whole_rhs = gather_wait(2 * a)
        x = dot_t(whole_rhs, top_lower_inv[a]).astype(BF16)
        forward.append(x)
        if a + 1 < levels:
            gather_send(2 * a + 1, x)
            base = col_finish(a + 1) - pending.get(a + 1, 0.0)
            if a == 0:
                loads[6].wait()
                loads[7].wait()
            gathered.append(gather_wait(2 * a + 1))
            target[a + 1] = base - dot_t(gathered[a], top_lower_blocks[pair_index(a + 1, a)])

    rhs = forward[levels - 1]
    upper = {a: forward[a].astype(F32) for a in range(levels)}
    last = None
    for a in range(levels - 1, -1, -1):
        gather_send(forward_steps + a, rhs)
        if last is not None:
            whole_send(a + 1)
            for l in range(a):
                upper[l] = upper[l] - dot_t(last, top_upper_blocks[pair_index(a + 1, l)])
        whole_rhs = gather_wait(forward_steps + a)
        solution_part = dot_t(whole_rhs, top_upper_inv[a]).astype(BF16)
        solved_send(a, solution_part)
        if a == levels - 1:
            loads[8].wait()
            loads[9].wait()
        last = solved_wait(a)
        if a > 0:
            rhs = (upper[a - 1] - dot_t(last, top_upper_blocks[pair_index(a, a - 1)])).astype(BF16)
    whole_send(0)

    def write_top(a):
        whole_wait(a)
        own = jnp.concatenate([whole[k, a * group + d] for k in range(n_gz)], axis=0)
        top_out[a] = own.astype(F32).T

    for a in range(levels - 1, 0, -1):
        write_top(a)
    whole_wait(0)
    picked = jnp.concatenate(
        [
            jnp.concatenate([whole[k, coupled_ref[0, j]] for k in range(n_gz)], axis=0)
            for j in range(couplings)
        ],
        axis=1,
    )
    back = solved_t[...].astype(F32) - dot_t(picked, leaf_upper_panel[0])
    back = jnp.where(live, back, 0.0).astype(BF16)
    answer = dot_t(leaf_upper_inv[0], back)
    live_rows = lax.broadcasted_iota(jnp.int32, (leaf_width, 1), 0) < tiles_ref[0] * TILE
    leaf_out[0] = jnp.where(live_rows, answer, 0.0)
    own = jnp.concatenate([whole[k, d] for k in range(n_gz)], axis=0)
    top_out[0] = own.astype(F32).T

    for a in range(levels):
        if n_row > 1:
            wait_bytes(row_in.at[a, pl.ds(0, n_row - 1)], row_sems.at[0, a])
        if n_gz > 1:
            wait_bytes(gz_in.at[a, pl.ds(0, n_gz - 1)], gz_sems.at[0, a])
            wait_bytes(whole.at[pl.ds(0, n_gz - 1), pl.ds(a * group, group)], whole_sems.at[0, a])
        if n_col > 1:
            wait_bytes(col_in.at[a, pl.ds(0, n_col - 1)], col_sems.at[0, a])
    if group > 1:
        for s in range(4 * levels - 1):
            wait_bytes(rings.at[0, pl.ds(0, group - 1)], gather_sems.at[0, s])


def solution(mesh):
    n_gz, n_row, n_col = mesh.shape["gz"], mesh.shape["row"], mesh.shape["col"]
    group = n_row * n_col

    def body(
        leaf_probe,
        leaf_lower_inv,
        leaf_upper_inv,
        leaf_lower_panel,
        leaf_upper_panel,
        leaf_tiles,
        coupled,
        top_probe,
        top_lower_inv,
        top_lower_blocks,
        top_upper_inv,
        top_upper_blocks,
    ):
        leaves, leaf_width, columns = leaf_probe.shape
        levels, sep_rows, _ = top_probe.shape
        couplings = coupled.shape[1]
        part = columns // n_gz
        assert leaves == 1 and sep_rows == TILE and part * n_gz == columns
        big = [
            leaf_probe,
            leaf_lower_inv,
            leaf_lower_panel,
            top_probe,
            top_lower_inv,
            top_lower_blocks,
            top_upper_inv,
            top_upper_blocks,
            leaf_upper_panel,
            leaf_upper_inv,
        ]
        sizes = (levels, n_gz, n_row, n_col, part, couplings, leaf_width)
        dma = pltpu.SemaphoreType.DMA
        smem = pl.BlockSpec(memory_space=pltpu.SMEM)
        vmem = pl.BlockSpec(memory_space=pltpu.VMEM)
        anywhere = pl.BlockSpec(memory_space=pl.ANY)
        scratch = [pltpu.VMEM(x.shape, x.dtype) for x in big] + [
            pltpu.VMEM((columns, leaf_width), BF16),
            pltpu.VMEM((couplings + 1, columns, TILE), BF16),
            pltpu.VMEM((levels, n_gz, part, TILE), F32),
            pltpu.VMEM((levels, n_row, n_gz, n_col, part, TILE), BF16),
            pltpu.VMEM((levels, n_row, n_gz, n_col, part, TILE), BF16),
            pltpu.VMEM((levels, n_gz, n_col, part, TILE), BF16),
            pltpu.VMEM((levels, n_gz, n_col, part, TILE), BF16),
            pltpu.VMEM((levels, n_col, part, TILE), BF16),
            pltpu.VMEM((levels, n_col, part, TILE), BF16),
            pltpu.VMEM((3 * levels - 1, group, part, TILE), BF16),
            pltpu.VMEM((n_gz, levels * group, part, TILE), BF16),
            dma((len(big),)),
            dma((2, levels)),
            dma((2, levels)),
            dma((2, levels)),
            dma((2, 4 * levels - 1)),
            dma((2, levels)),
        ]
        return pl.pallas_call(
            functools.partial(kernel, sizes),
            out_shape=(
                jax.ShapeDtypeStruct(leaf_probe.shape, F32),
                jax.ShapeDtypeStruct(top_probe.shape, F32),
            ),
            in_specs=[smem, smem] + [anywhere] * len(big),
            out_specs=(vmem, vmem),
            scratch_shapes=scratch,
            compiler_params=pltpu.CompilerParams(
                collective_id=0, has_side_effects=True, vmem_limit_bytes=56 * 2**20
            ),
        )(leaf_tiles, coupled, *big)

    leaf3 = P(("gz", "row", "col"), None, None)
    top3 = P(None, ("row", "col"), None)
    return jax.shard_map(
        body,
        mesh=mesh,
        in_specs=(
            leaf3,
            leaf3,
            leaf3,
            leaf3,
            leaf3,
            P(("gz", "row", "col")),
            P(("gz", "row", "col"), None),
            top3,
            top3,
            top3,
            top3,
            top3,
        ),
        out_specs=(leaf3, top3),
        check_vma=False,
    )
```

time: 475 us -> 87.1 us (0.18)
  blocking collectives: 355 us -> 0 us
  Pallas kernels: 0 us -> 82.3 us
  waiting for transfers between devices: 82.1 us -> 0 us
  between operations: 15 us -> 1.29 us
  matrix products: 10.4 us -> 0 us
    all_gather x15 -> x0, blocking collectives: 355 us -> none  [the longest x8 194 us: solve_level(): lax.all_gather(target, ('row', 'col'), axis=0, tiled=True)]
    pallas_call x0 -> x1, Pallas kernels: none -> 82.3 us  [body(): pl.pallas_call(functools.partial(kernel, sizes), out_shape=(jax.ShapeDtyp...]
    psum x1 -> x0, waiting for transfers between devices: 43.7 us -> none  [layer_reduce(): lax.psum(partial_value.astype(jnp.bfloat16), 'gz').astype(jnp.float32)]
    reduce_scatter x1 -> x0, waiting for transfers between devices: 38.4 us -> none  [body(): lax.psum_scatter(update.astype(jnp.bfloat16), ('row', 'col'), scatter_dim...]
    dot_general x23 -> x0, matrix products: 10.4 us -> none  [the longest x8 2.94 us: solve_level(): jnp.dot(inverse, lax.all_gather(target, ('row', 'col'), axis=0, tiled=Tru...]
  transfers between devices with their start and end apart: 2 -> 0, of which waited for: 2 -> 0; matrix products, arithmetic and copies ran while one was open for 0% -> 0% of each run, Pallas kernels for 0% -> 0%
where the time goes in v1:
time: 87.1 us; the launch traced here: 86.9 us
  Pallas kernels  82.3 us (94%)
  local copies, waits for them, and re-layouts  3.34 us (4%)
  between operations  1.29 us (1%)
    pallas_call x1, Pallas kernels, body(): pl.pallas_call(functools.partial(kernel, sizes), out_shape=(jax.ShapeDtyp...  82.3 us
    unnamed x2, local copies, waits for them, and re-layouts  3.34 us

profile of v1, /device:TPU:0, one launch (start us, length us, event | category | flops | bytes accessed | tf_op | source)
XLA Modules:
  0.0 86.9 jit_solution(9270794271372635614)
XLA Ops:
  1.3 82.3 %shard_map.131 = (f32[1,512,128]{2,1,0:T(8,128)}, f32[4,128,128]{2,1,0:T(8,128)}) custom-call(s32[1]{0:T(128)S(6)} %copy.16.tiles_ref, s32[1,8]{1,0:T(1,128)} %coupled_ref.1, bf16[1,512,128]{2,1,0:T(8,128)(2,1)} %leaf_probe_hbm.1, bf16[1,512,512]{2,1,0:T(8,128)(2,1)} %leaf_lower_inv_hbm.1, bf16[1,1024,512]{2,1,0:T(8,128)(2,1)} %leaf_lower_panel_hbm.1, ...), custom_call_target="tpu_custom_call" | custom-call | tf_op jit(solution)/shard_map/pallas_call | solution.py:393
  83.6 1.7 %copy.17 = f32[1,512,128]{2,1,0:T(8,128)} copy(f32[1,512,128]{2,1,0:T(8,128)} %get-tuple-element.4) | data formatting | bytes 524288
  85.2 1.7 %copy.18 = f32[4,128,128]{2,1,0:T(8,128)} copy(f32[4,128,128]{2,1,0:T(8,128)} %get-tuple-element.5) | data formatting | bytes 524288

commit v2 on v1

--- a/solution.py
+++ b/solution.py
@@ -58,16 +58,21 @@
     rings,
     whole,
     load_sem,
+    pair_sems,
     row_sems,
     gz_sems,
     col_sems,
     gather_sems,
     whole_sems,
 ):
-    levels, n_gz, n_row, n_col, part, couplings, leaf_width = sizes
+    levels, n_gz, n_row, n_col, pair, part, couplings, leaf_width = sizes
     group = n_row * n_col
+    teams, parts = group // pair, n_gz * pair
     g, r, c = lax.axis_index("gz"), lax.axis_index("row"), lax.axis_index("col")
     d = r * n_col + c
+    base_row, q = lax.div(r, pair) * pair, lax.rem(r, pair)
+    team = lax.div(r, pair) * n_col + c
+    piece = g * pair + q
     forward_steps = 2 * levels - 1
 
     sources = [
@@ -82,8 +87,10 @@
         (leaf_upper_panel_hbm, leaf_upper_panel),
         (leaf_upper_inv_hbm, leaf_upper_inv),
     ]
+    shared = range(3, 8)
     loads = [
-        pltpu.make_async_copy(src, dst, load_sem.at[i]) for i, (src, dst) in enumerate(sources)
+        pltpu.make_async_copy(src, dst.at[:, q] if i in shared else dst, load_sem.at[i])
+        for i, (src, dst) in enumerate(sources)
     ]
     for load in loads:
         load.start()
@@ -100,11 +107,24 @@
     def gz_peer(i):
         return (lax.rem(g + i, n_gz), r, c)
 
+    def team_peer(i):
+        peer = lax.rem(team + i, teams)
+        return (g, lax.div(peer, n_col) * pair + q, lax.rem(peer, n_col))
+
+    def piece_peer(i):
+        peer = lax.rem(piece + i, parts)
+        return (lax.div(peer, pair), base_row + lax.rem(peer, pair), c)
+
+    def far_peer(i):
+        at = i - 1
+        layer = lax.rem(g + 1 + lax.div(at, pair), n_gz)
+        return (layer, base_row + lax.rem(at, pair), c)
+
     def greet(device):
         pl.semaphore_signal(barrier, inc=1, device_id=device, device_id_type=pl.DeviceIdType.MESH)
 
     each(group, lambda i: greet(group_peer(i)))
-    each(n_gz, lambda i: greet(gz_peer(i)))
+    each((n_gz - 1) * pair + 1, lambda i: greet(far_peer(i)))
 
     def send(src, dst, sems, at, device):
         pltpu.make_async_remote_copy(
@@ -119,6 +139,31 @@
     def wait_bytes(ref, sem):
         pltpu.make_async_copy(ref, ref, sem).wait()
 
+    def pair_send(w):
+        src, dst = sources[w]
+
+        def step(i):
+            to = (g, base_row + lax.rem(q + i, pair), c)
+            send(src, dst.at[:, q], pair_sems, w - shared[0], to)
+
+        each(pair, step)
+
+    def ready(w):
+        loads[w].wait()
+        if pair > 1:
+            ref = sources[w][1]
+            wait_bytes(ref.at[:, pl.ds(0, pair - 1)], pair_sems.at[1, w - shared[0]])
+
+    def weight(ref, at):
+        return ref[at].reshape(pair * TILE, ref.shape[-1])
+
+    def side_by_side(value):
+        return jnp.concatenate([value[k] for k in range(pair)], axis=1)
+
+    def in_order(block):
+        order = [(t // n_col, t % n_col) for t in range(group)]
+        return jnp.concatenate([block(x // pair * n_col + y, x % pair) for x, y in order], axis=1)
+
     def row_send(a):
         def step(i):
             other = lax.rem(r + i, n_row)
@@ -162,47 +207,51 @@
         total = gz_sum[a, c].astype(F32)
         for i in range(1, n_col):
             total = total + col_in[a, lax.rem(c + i, n_col)].astype(F32)
-        return probe_t[a, g] - total
+        return side_by_side(probe_t[a, :, piece] - total)
 
     def gather_send(step_at, value):
-        rings[step_at, d] = value
-
-        def step(i):
-            send(rings.at[step_at, d], rings.at[step_at, d], gather_sems, step_at, group_peer(i))
-
-        each(group, step)
+        for k in range(pair):
+            rings[step_at, team, k] = value[:, k * TILE : (k + 1) * TILE]
+
+        def step(i):
+            own = rings.at[step_at, team]
+            send(own, own, gather_sems, step_at, team_peer(i))
+
+        each(teams, step)
 
     def gather_wait(step_at):
-        if group > 1:
-            wait_bytes(rings.at[step_at, pl.ds(0, group - 1)], gather_sems.at[1, step_at])
-        return jnp.concatenate([rings[step_at, i] for i in range(group)], axis=1)
+        if teams > 1:
+            wait_bytes(rings.at[step_at, pl.ds(0, teams - 1)], gather_sems.at[1, step_at])
+        return in_order(lambda at, k: rings[step_at, at, k])
 
     def solved_send(a, value):
-        at = a * group + d
-        whole[g, at] = value
-
-        def step(i):
-            send(whole.at[g, at], whole.at[g, at], gather_sems, 3 * levels - 1 + a, group_peer(i))
-
-        each(group, step)
+        at = a * teams + team
+        for k in range(pair):
+            whole[piece, at, k] = value[:, k * TILE : (k + 1) * TILE]
+
+        def step(i):
+            own = whole.at[piece, at]
+            send(own, own, gather_sems, 3 * levels - 1 + a, team_peer(i))
+
+        each(teams, step)
 
     def solved_wait(a):
-        if group > 1:
+        if teams > 1:
             wait_bytes(
-                whole.at[g, pl.ds(a * group, group - 1)], gather_sems.at[1, 3 * levels - 1 + a]
+                whole.at[piece, pl.ds(a * teams, teams - 1)], gather_sems.at[1, 3 * levels - 1 + a]
             )
-        return jnp.concatenate([whole[g, a * group + i] for i in range(group)], axis=1)
+        return in_order(lambda at, k: whole[piece, a * teams + at, k])
 
     def whole_send(a):
         def step(i):
-            at = pl.ds(a * group, group)
-            send(whole.at[g, at], whole.at[g, at], whole_sems, a, gz_peer(i))
-
-        each(n_gz, step)
+            own = whole.at[piece, pl.ds(a * teams, teams)]
+            send(own, own, whole_sems, a, piece_peer(i))
+
+        each(parts, step)
 
     def whole_wait(a):
-        if n_gz > 1:
-            wait_bytes(whole.at[pl.ds(0, n_gz - 1), pl.ds(a * group, group)], whole_sems.at[1, a])
+        if parts > 1:
+            wait_bytes(whole.at[pl.ds(0, parts - 1), pl.ds(a * teams, teams)], whole_sems.at[1, a])
 
     live = lax.broadcasted_iota(jnp.int32, (1, leaf_width), 1) < tiles_ref[0] * TILE
     loads[0].wait()
@@ -210,6 +259,9 @@
     loads[1].wait()
     solved = jnp.where(live, dot_t(masked, leaf_lower_inv[0]), 0.0).astype(BF16)
     solved_t[...] = solved
+    pl.semaphore_wait(barrier, group - 1 + (n_gz - 1) * pair)
+    for w in (3, 4, 5):
+        pair_send(w)
     loads[2].wait()
     for j in range(couplings):
         rows = leaf_lower_panel[0, pl.ds(j * TILE, TILE), :]
@@ -223,30 +275,34 @@
                 at = jnp.where(coupled_ref[0, j] == a * group + t, j, at)
             block = blocks_t[at]
             t_row, t_col = lax.div(t, n_col), lax.rem(t, n_col)
-            for k in range(n_gz):
-                upd[a, t_row, k, t_col] = block[k * part : (k + 1) * part]
+            first, place_in = lax.div(t_row, pair) * pair, lax.rem(t_row, pair)
+            for k in range(parts):
+                lines = block[k * part : (k + 1) * part]
+                upd[a, first + k % pair, k // pair, t_col, place_in] = lines
             return carry
 
         lax.fori_loop(0, group, place, 0)
 
     spread(0)
-    pl.semaphore_wait(barrier, group - 1 + n_gz - 1)
     row_send(0)
     for a in range(1, levels):
         spread(a)
         row_send(a)
     row_finish(0)
     gz_send(0)
-    loads[3].wait()
+    ready(3)
     for a in range(levels):
-        probe_t[a] = top_probe[a].astype(F32).T.reshape(probe_t.shape[1:])
+        for k in range(pair):
+            probe_t[a, k] = top_probe[a, k].astype(F32).T.reshape(probe_t.shape[2:])
     for a in range(1, levels):
         row_finish(a)
         gz_send(a)
     gz_finish(0)
     col_send(0)
-    loads[4].wait()
-    loads[5].wait()
+    for w in (6, 7):
+        pair_send(w)
+    ready(4)
+    ready(5)
     target = {0: col_finish(0)}
 
     forward = []
@@ -259,22 +315,21 @@
             for h in range(a + 1, levels):
                 known = [l for l in range(levels) if l == a - 1]
                 for l in known:
-                    pending[h] = pending.get(h, 0.0) + dot_t(gathered[l], top_lower_blocks[pair_index(h, l)])
+                    pending[h] = pending.get(h, 0.0) + dot_t(gathered[l], weight(top_lower_blocks, pair_index(h, l)))
         else:
             gathered = []
             pending = {}
         whole_rhs = gather_wait(2 * a)
-        x = dot_t(whole_rhs, top_lower_inv[a]).astype(BF16)
+        x = dot_t(whole_rhs, weight(top_lower_inv, a)).astype(BF16)
         forward.append(x)
         if a + 1 < levels:
             gather_send(2 * a + 1, x)
             base = col_finish(a + 1) - pending.get(a + 1, 0.0)
-            if a == 0:
-                loads[6].wait()
-                loads[7].wait()
             gathered.append(gather_wait(2 * a + 1))
-            target[a + 1] = base - dot_t(gathered[a], top_lower_blocks[pair_index(a + 1, a)])
-
+            target[a + 1] = base - dot_t(gathered[a], weight(top_lower_blocks, pair_index(a + 1, a)))
+
+    ready(6)
+    ready(7)
     rhs = forward[levels - 1]
     upper = {a: forward[a].astype(F32) for a in range(levels)}
     last = None
@@ -283,29 +338,35 @@
         if last is not None:
             whole_send(a + 1)
             for l in range(a):
-                upper[l] = upper[l] - dot_t(last, top_upper_blocks[pair_index(a + 1, l)])
+                upper[l] = upper[l] - dot_t(last, weight(top_upper_blocks, pair_index(a + 1, l)))
         whole_rhs = gather_wait(forward_steps + a)
-        solution_part = dot_t(whole_rhs, top_upper_inv[a]).astype(BF16)
+        solution_part = dot_t(whole_rhs, weight(top_upper_inv, a)).astype(BF16)
         solved_send(a, solution_part)
         if a == levels - 1:
             loads[8].wait()
             loads[9].wait()
         last = solved_wait(a)
         if a > 0:
-            rhs = (upper[a - 1] - dot_t(last, top_upper_blocks[pair_index(a, a - 1)])).astype(BF16)
+            rhs = (upper[a - 1] - dot_t(last, weight(top_upper_blocks, pair_index(a, a - 1)))).astype(BF16)
     whole_send(0)
 
     def write_top(a):
         whole_wait(a)
-        own = jnp.concatenate([whole[k, a * group + d] for k in range(n_gz)], axis=0)
+        own = jnp.concatenate([whole[k, a * teams + team, q] for k in range(parts)], axis=0)
         top_out[a] = own.astype(F32).T
 
     for a in range(levels - 1, 0, -1):
         write_top(a)
     whole_wait(0)
+
+    def where(tile):
+        level, t = lax.div(tile, group), lax.rem(tile, group)
+        x, y = lax.div(t, n_col), lax.rem(t, n_col)
+        return level * teams + lax.div(x, pair) * n_col + y, lax.rem(x, pair)
+
     picked = jnp.concatenate(
         [
-            jnp.concatenate([whole[k, coupled_ref[0, j]] for k in range(n_gz)], axis=0)
+            jnp.concatenate([whole[(k, *where(coupled_ref[0, j]))] for k in range(parts)], axis=0)
             for j in range(couplings)
         ],
         axis=1,
@@ -315,7 +376,7 @@
     answer = dot_t(leaf_upper_inv[0], back)
     live_rows = lax.broadcasted_iota(jnp.int32, (leaf_width, 1), 0) < tiles_ref[0] * TILE
     leaf_out[0] = jnp.where(live_rows, answer, 0.0)
-    own = jnp.concatenate([whole[k, d] for k in range(n_gz)], axis=0)
+    own = jnp.concatenate([whole[k, team, q] for k in range(parts)], axis=0)
     top_out[0] = own.astype(F32).T
 
     for a in range(levels):
@@ -323,12 +384,17 @@
             wait_bytes(row_in.at[a, pl.ds(0, n_row - 1)], row_sems.at[0, a])
         if n_gz > 1:
             wait_bytes(gz_in.at[a, pl.ds(0, n_gz - 1)], gz_sems.at[0, a])
-            wait_bytes(whole.at[pl.ds(0, n_gz - 1), pl.ds(a * group, group)], whole_sems.at[0, a])
+        if parts > 1:
+            wait_bytes(whole.at[pl.ds(0, parts - 1), pl.ds(a * teams, teams)], whole_sems.at[0, a])
         if n_col > 1:
             wait_bytes(col_in.at[a, pl.ds(0, n_col - 1)], col_sems.at[0, a])
-    if group > 1:
+    if teams > 1:
         for s in range(4 * levels - 1):
-            wait_bytes(rings.at[0, pl.ds(0, group - 1)], gather_sems.at[0, s])
+            wait_bytes(rings.at[0, pl.ds(0, teams - 1)], gather_sems.at[0, s])
+    if pair > 1:
+        for w in shared:
+            ref = sources[w][1]
+            wait_bytes(ref.at[:, pl.ds(0, pair - 1)], pair_sems.at[0, w - shared[0]])
 
 
 def solution(mesh):
@@ -352,8 +418,12 @@
         leaves, leaf_width, columns = leaf_probe.shape
         levels, sep_rows, _ = top_probe.shape
         couplings = coupled.shape[1]
-        part = columns // n_gz
-        assert leaves == 1 and sep_rows == TILE and part * n_gz == columns
+        weights = (top_lower_inv, top_lower_blocks, top_upper_inv, top_upper_blocks)
+        small = sum(x.size * x.dtype.itemsize for x in weights) <= 12 * 2**20
+        pair = 2 if small and n_row % 2 == 0 and columns % (n_gz * 32) == 0 else 1
+        teams, parts = group // pair, n_gz * pair
+        part = columns // parts
+        assert leaves == 1 and sep_rows == TILE and part * parts == columns
         big = [
             leaf_probe,
             leaf_lower_inv,
@@ -366,24 +436,29 @@
             leaf_upper_panel,
             leaf_upper_inv,
         ]
-        sizes = (levels, n_gz, n_row, n_col, part, couplings, leaf_width)
+        sizes = (levels, n_gz, n_row, n_col, pair, part, couplings, leaf_width)
         dma = pltpu.SemaphoreType.DMA
         smem = pl.BlockSpec(memory_space=pltpu.SMEM)
         vmem = pl.BlockSpec(memory_space=pltpu.VMEM)
         anywhere = pl.BlockSpec(memory_space=pl.ANY)
-        scratch = [pltpu.VMEM(x.shape, x.dtype) for x in big] + [
+        held = [
+            (x.shape[0], pair, *x.shape[1:]) if i in range(3, 8) else x.shape
+            for i, x in enumerate(big)
+        ]
+        scratch = [pltpu.VMEM(shape, x.dtype) for shape, x in zip(held, big)] + [
             pltpu.VMEM((columns, leaf_width), BF16),
             pltpu.VMEM((couplings + 1, columns, TILE), BF16),
-            pltpu.VMEM((levels, n_gz, part, TILE), F32),
-            pltpu.VMEM((levels, n_row, n_gz, n_col, part, TILE), BF16),
-            pltpu.VMEM((levels, n_row, n_gz, n_col, part, TILE), BF16),
-            pltpu.VMEM((levels, n_gz, n_col, part, TILE), BF16),
-            pltpu.VMEM((levels, n_gz, n_col, part, TILE), BF16),
-            pltpu.VMEM((levels, n_col, part, TILE), BF16),
-            pltpu.VMEM((levels, n_col, part, TILE), BF16),
-            pltpu.VMEM((3 * levels - 1, group, part, TILE), BF16),
-            pltpu.VMEM((n_gz, levels * group, part, TILE), BF16),
+            pltpu.VMEM((levels, pair, parts, part, TILE), F32),
+            pltpu.VMEM((levels, n_row, n_gz, n_col, pair, part, TILE), BF16),
+            pltpu.VMEM((levels, n_row, n_gz, n_col, pair, part, TILE), BF16),
+            pltpu.VMEM((levels, n_gz, n_col, pair, part, TILE), BF16),
+            pltpu.VMEM((levels, n_gz, n_col, pair, part, TILE), BF16),
+            pltpu.VMEM((levels, n_col, pair, part, TILE), BF16),
+            pltpu.VMEM((levels, n_col, pair, part, TILE), BF16),
+            pltpu.VMEM((3 * levels - 1, teams, pair, part, TILE), BF16),
+            pltpu.VMEM((parts, levels * teams, pair, part, TILE), BF16),
             dma((len(big),)),
+            dma((2, 5)),
             dma((2, levels)),
             dma((2, levels)),
             dma((2, levels)),

time: 87.1 us -> 88.1 us (1.011)
  Pallas kernels: 82.3 us -> 83.3 us
    pallas_call x1, Pallas kernels: 82.3 us -> 83.3 us  [body(): pl.pallas_call(functools.partial(kernel, sizes), out_shape=(jax.ShapeDtyp...]
where the time goes in v2:
time: 88.1 us; the launch traced here: 87.9 us
  Pallas kernels  83.3 us (95%)
  local copies, waits for them, and re-layouts  3.34 us (4%)
  between operations  1.29 us (1%)
    pallas_call x1, Pallas kernels, body(): pl.pallas_call(functools.partial(kernel, sizes), out_shape=(jax.ShapeDtyp...  83.3 us
    unnamed x2, local copies, waits for them, and re-layouts  3.34 us

profile of v2, /device:TPU:0, one launch (start us, length us, event | category | flops | bytes accessed | tf_op | source)
XLA Modules:
  0.0 87.9 jit_solution(16506394524392596585)
XLA Ops:
  1.3 83.3 %shard_map.131 = (f32[1,512,128]{2,1,0:T(8,128)}, f32[4,128,128]{2,1,0:T(8,128)}) custom-call(s32[1]{0:T(128)S(6)} %copy.16.tiles_ref, s32[1,8]{1,0:T(1,128)} %coupled_ref.1, bf16[1,512,128]{2,1,0:T(8,128)(2,1)} %leaf_probe_hbm.1, bf16[1,512,512]{2,1,0:T(8,128)(2,1)} %leaf_lower_inv_hbm.1, bf16[1,1024,512]{2,1,0:T(8,128)(2,1)} %leaf_lower_panel_hbm.1, ...), custom_call_target="tpu_custom_call" | custom-call | tf_op jit(solution)/shard_map/pallas_call | solution.py:468
  84.6 1.7 %copy.17 = f32[1,512,128]{2,1,0:T(8,128)} copy(f32[1,512,128]{2,1,0:T(8,128)} %get-tuple-element.4) | data formatting | bytes 524288
  86.3 1.7 %copy.18 = f32[4,128,128]{2,1,0:T(8,128)} copy(f32[4,128,128]{2,1,0:T(8,128)} %get-tuple-element.5) | data formatting | bytes 524288

commit v3 on v2

--- a/solution.py
+++ b/solution.py
@@ -18,6 +18,10 @@
 
 def dot_t(left, right):
     return lax.dot_general(left, right, (((1,), (1,)), ((), ())), preferred_element_type=F32)
+
+
+def dot_few(few, matrix):
+    return dot_t(matrix, few).T
 
 
 def kernel(
@@ -315,18 +319,18 @@
             for h in range(a + 1, levels):
                 known = [l for l in range(levels) if l == a - 1]
                 for l in known:
-                    pending[h] = pending.get(h, 0.0) + dot_t(gathered[l], weight(top_lower_blocks, pair_index(h, l)))
+                    pending[h] = pending.get(h, 0.0) + dot_few(gathered[l], weight(top_lower_blocks, pair_index(h, l)))
         else:
             gathered = []
             pending = {}
         whole_rhs = gather_wait(2 * a)
-        x = dot_t(whole_rhs, weight(top_lower_inv, a)).astype(BF16)
+        x = dot_few(whole_rhs, weight(top_lower_inv, a)).astype(BF16)
         forward.append(x)
         if a + 1 < levels:
             gather_send(2 * a + 1, x)
             base = col_finish(a + 1) - pending.get(a + 1, 0.0)
             gathered.append(gather_wait(2 * a + 1))
-            target[a + 1] = base - dot_t(gathered[a], weight(top_lower_blocks, pair_index(a + 1, a)))
+            target[a + 1] = base - dot_few(gathered[a], weight(top_lower_blocks, pair_index(a + 1, a)))
 
     ready(6)
     ready(7)
@@ -338,16 +342,16 @@
         if last is not None:
             whole_send(a + 1)
             for l in range(a):
-                upper[l] = upper[l] - dot_t(last, weight(top_upper_blocks, pair_index(a + 1, l)))
+                upper[l] = upper[l] - dot_few(last, weight(top_upper_blocks, pair_index(a + 1, l)))
         whole_rhs = gather_wait(forward_steps + a)
-        solution_part = dot_t(whole_rhs, weight(top_upper_inv, a)).astype(BF16)
+        solution_part = dot_few(whole_rhs, weight(top_upper_inv, a)).astype(BF16)
         solved_send(a, solution_part)
         if a == levels - 1:
             loads[8].wait()
             loads[9].wait()
         last = solved_wait(a)
         if a > 0:
-            rhs = (upper[a - 1] - dot_t(last, weight(top_upper_blocks, pair_index(a, a - 1)))).astype(BF16)
+            rhs = (upper[a - 1] - dot_few(last, weight(top_upper_blocks, pair_index(a, a - 1)))).astype(BF16)
     whole_send(0)
 
     def write_top(a):

time: 88.1 us -> 88.9 us (level)
  no operation moved by 1% of the time
where the time goes in v3:
time: 88.9 us; the launch traced here: 88.7 us
  Pallas kernels  84 us (94%)
  local copies, waits for them, and re-layouts  3.34 us (4%)
  between operations  1.29 us (1%)
    pallas_call x1, Pallas kernels, body(): pl.pallas_call(functools.partial(kernel, sizes), out_shape=(jax.ShapeDtyp...  84 us
    unnamed x2, local copies, waits for them, and re-layouts  3.34 us

profile of v3, /device:TPU:0, one launch (start us, length us, event | category | flops | bytes accessed | tf_op | source)
XLA Modules:
  0.0 88.7 jit_solution(4269817299521480034)
XLA Ops:
  1.3 84.0 %shard_map.131 = (f32[1,512,128]{2,1,0:T(8,128)}, f32[4,128,128]{2,1,0:T(8,128)}) custom-call(s32[1]{0:T(128)S(6)} %copy.16.tiles_ref, s32[1,8]{1,0:T(1,128)} %coupled_ref.1, bf16[1,512,128]{2,1,0:T(8,128)(2,1)} %leaf_probe_hbm.1, bf16[1,512,512]{2,1,0:T(8,128)(2,1)} %leaf_lower_inv_hbm.1, bf16[1,1024,512]{2,1,0:T(8,128)(2,1)} %leaf_lower_panel_hbm.1, ...), custom_call_target="tpu_custom_call" | custom-call | tf_op jit(solution)/shard_map/pallas_call | solution.py:472
  85.3 1.7 %copy.17 = f32[1,512,128]{2,1,0:T(8,128)} copy(f32[1,512,128]{2,1,0:T(8,128)} %get-tuple-element.4) | data formatting | bytes 524288
  87.0 1.7 %copy.18 = f32[4,128,128]{2,1,0:T(8,128)} copy(f32[4,128,128]{2,1,0:T(8,128)} %get-tuple-element.5) | data formatting | bytes 524288

commit v4 on v1

--- a/solution.py
+++ b/solution.py
@@ -85,7 +85,7 @@
     loads = [
         pltpu.make_async_copy(src, dst, load_sem.at[i]) for i, (src, dst) in enumerate(sources)
     ]
-    for load in loads:
+    for load in loads[:3]:
         load.start()
 
     def each(count, step):
@@ -211,6 +211,8 @@
     solved = jnp.where(live, dot_t(masked, leaf_lower_inv[0]), 0.0).astype(BF16)
     solved_t[...] = solved
     loads[2].wait()
+    for load in loads[3:]:
+        load.start()
     for j in range(couplings):
         rows = leaf_lower_panel[0, pl.ds(j * TILE, TILE), :]
         blocks_t[j] = dot_t(solved, rows).astype(BF16)
@@ -232,19 +234,22 @@
     spread(0)
     pl.semaphore_wait(barrier, group - 1 + n_gz - 1)
     row_send(0)
-    for a in range(1, levels):
+    if levels > 1:
+        spread(1)
+        row_send(1)
+    row_finish(0)
+    gz_send(0)
+    for a in range(2, levels):
         spread(a)
         row_send(a)
-    row_finish(0)
-    gz_send(0)
     loads[3].wait()
     for a in range(levels):
         probe_t[a] = top_probe[a].astype(F32).T.reshape(probe_t.shape[1:])
-    for a in range(1, levels):
-        row_finish(a)
-        gz_send(a)
     gz_finish(0)
     col_send(0)
+    if levels > 1:
+        row_finish(1)
+        gz_send(1)
     loads[4].wait()
     loads[5].wait()
     target = {0: col_finish(0)}
@@ -255,6 +260,9 @@
         if a + 1 < levels:
             gz_finish(a + 1)
             col_send(a + 1)
+        if a + 2 < levels:
+            row_finish(a + 2)
+            gz_send(a + 2)
         if a >= 1:
             for h in range(a + 1, levels):
                 known = [l for l in range(levels) if l == a - 1]
@@ -298,7 +306,7 @@
     def write_top(a):
         whole_wait(a)
         own = jnp.concatenate([whole[k, a * group + d] for k in range(n_gz)], axis=0)
-        top_out[a] = own.astype(F32).T
+        top_out[a] = own.astype(F32).T.astype(BF16)
 
     for a in range(levels - 1, 0, -1):
         write_top(a)
@@ -316,7 +324,7 @@
     live_rows = lax.broadcasted_iota(jnp.int32, (leaf_width, 1), 0) < tiles_ref[0] * TILE
     leaf_out[0] = jnp.where(live_rows, answer, 0.0)
     own = jnp.concatenate([whole[k, d] for k in range(n_gz)], axis=0)
-    top_out[0] = own.astype(F32).T
+    top_out[0] = own.astype(F32).T.astype(BF16)
 
     for a in range(levels):
         if n_row > 1:
@@ -390,11 +398,11 @@
             dma((2, 4 * levels - 1)),
             dma((2, levels)),
         ]
-        return pl.pallas_call(
+        leaf, top = pl.pallas_call(
             functools.partial(kernel, sizes),
             out_shape=(
                 jax.ShapeDtypeStruct(leaf_probe.shape, F32),
-                jax.ShapeDtypeStruct(top_probe.shape, F32),
+                jax.ShapeDtypeStruct(top_probe.shape, BF16),
             ),
             in_specs=[smem, smem] + [anywhere] * len(big),
             out_specs=(vmem, vmem),
@@ -403,6 +411,7 @@
                 collective_id=0, has_side_effects=True, vmem_limit_bytes=56 * 2**20
             ),
         )(leaf_tiles, coupled, *big)
+        return leaf, top.astype(F32)
 
     leaf3 = P(("gz", "row", "col"), None, None)
     top3 = P(None, ("row", "col"), None)

time: 87.1 us -> 86.8 us (level)
  local copies, waits for them, and re-layouts: 3.34 us -> 1.67 us
  other arithmetic: 0 us -> 1.63 us
    unnamed x2 -> x1, local copies, waits for them, and re-layouts: 3.34 us -> 1.67 us
    convert_element_type x0 -> x1, other arithmetic: none -> 1.63 us  [body(): return (leaf, top.astype(F32))]
where the time goes in v4:
time: 86.8 us; the launch traced here: 86.6 us
  Pallas kernels  82 us (94%)
  local copies, waits for them, and re-layouts  1.67 us (2%)
  other arithmetic  1.63 us (2%)
  between operations  1.29 us (1%)
    pallas_call x1, Pallas kernels, body(): pl.pallas_call(functools.partial(kernel, sizes), out_shape=(jax.ShapeDtyp...  82 us

profile of v4, /device:TPU:0, one launch (start us, length us, event | category | flops | bytes accessed | tf_op | source)
XLA Modules:
  0.0 86.6 jit_solution(7480685714641104674)
XLA Ops:
  1.3 82.0 %shard_map.131 = (f32[1,512,128]{2,1,0:T(8,128)}, bf16[4,128,128]{2,1,0:T(8,128)(2,1)}) custom-call(s32[1]{0:T(128)S(6)} %copy.15.tiles_ref, s32[1,8]{1,0:T(1,128)} %coupled_ref.1, bf16[1,512,128]{2,1,0:T(8,128)(2,1)} %leaf_probe_hbm.1, bf16[1,512,512]{2,1,0:T(8,128)(2,1)} %leaf_lower_inv_hbm.1, bf16[1,1024,512]{2,1,0:T(8,128)(2,1)} %leaf_lower_panel_hbm.1, ...), custom_call_target="tpu_custom_call" | custom-call | tf_op jit(solution)/shard_map/pallas_call | solution.py:401
  83.3 1.6 %convert_element_type.3 = f32[4,128,128]{2,1,0:T(8,128)} convert(bf16[4,128,128]{2,1,0:T(8,128)(2,1)} %get-tuple-element.5) | non-fusion elementwise | flops 65536 | bytes 393216 | tf_op jit(solution)/shard_map/convert_element_type | solution.py:414
  84.9 1.7 %copy.16 = f32[1,512,128]{2,1,0:T(8,128)} copy(f32[1,512,128]{2,1,0:T(8,128)} %get-tuple-element.8) | data formatting | bytes 524288
